TPU v7x, 32 devices: a whole 2x2x4 slice. The times are simulated.
32 devices in a mesh: stack: 2 (over y), gx: 4 (over z), gy: 2 (over x), gz: 2 (over core).
Axes of the slice: x: 2, y: 2, z: 4, core: 2. Of those that a mesh axis runs over, the one named last changes fastest.
Arguments:
- initial_solid_warmth: float32 [16, 256, 512], P(('stack', 'gz'), 'gy', 'gx'), parts along dimension 0, may hold values from 0 to 1
- dissipated_power: float32 [16, 256, 512], P(('stack', 'gz'), 'gy', 'gx'), parts along dimension 0, may hold values from 0.1 to 2
- thermal_storage: float32 [16, 256, 512], P(('stack', 'gz'), 'gy', 'gx'), parts along dimension 0, may hold values from 0.1 to 1
- thermal_conductance_pair: float32 [2, 16, 256, 512], P(None, ('stack', 'gz'), 'gy', 'gx'), parts along dimension 1, may hold values from 0.3 to 3
- fluid_warmth: float32 [8, 128, 128], P(('stack', 'gy', 'gz'), 'gx'), parts along dimension 0, may hold values from 0 to 1
- exchange_coefficient: float32 [8, 128, 128], P(('stack', 'gy', 'gz'), 'gx'), parts along dimension 0, may hold values from 0.5 to 4
- channel_block_holder: int32 [4, 128, 1], replicated, may hold values from 0 to 3; in each aligned block of 32 rows (0 to 31, 32 to 63, ..., all dimensions but the last counted through in order) at most 16 rows name the same one
- channel_stratum_slot: int32 [4, 128], replicated, may hold values from 0 to 3
- channel_transverse_slot: int32 [4, 128], replicated, may hold values from 0 to 127
Outputs:
- temperature_out: float32 [16, 256, 512], P(('stack', 'gz'), 'gy', 'gx'), parts along dimension 0
- coolant_out: float32 [8, 128, 128], P(('stack', 'gy', 'gz'), 'gx'), parts along dimension 0
There are 2 independent parts, one for each index of `stack`. A program takes and returns all parts, laid end to end along the dimension named above; an argument that names none is the same for every part. Nothing has to cross between parts.
Inputs may be any that keep to these rules, and one draw needn't show every extreme that they name: `channel_block_holder`: within the 32 segments of one device (aligned blocks of 32 entries along the second dimension) no tile is named more than 16 times; some tile is named exactly 16 times.
All inputs are finite; a program needn't handle non-finite values.
Results may differ from a plain program's by a relative error of at most 0.00012.
Values sent between devices are 32-bit elements; how exact they have to be, the bound alone decides.
No kernel may reach another device: no remote copies, remote signals or barrier semaphores. Data moves between devices by JAX's collectives and lax.ppermute only.
A program may use at most 64 MiB of HBM per device.

v0:
```python
import functools

import jax
import jax.numpy as jnp
from jax import lax
from jax.experimental import pallas as pl
from jax.experimental.pallas import tpu as pltpu
from jax.sharding import PartitionSpec as P

STEPS = 2
ITERS = 4
HALO = STEPS * ITERS
GROUP = 2 * HALO
LANES = 128
RAW = 5
FIELDS = 7
coolant_gain = 0.5

VMEM = pl.BlockSpec(memory_space=pltpu.VMEM)
PARAMS = pltpu.CompilerParams(vmem_limit_bytes=40 * 1024 * 1024)


def cost(microseconds):
    return pl.CostEstimate(flops=0, bytes_accessed=int(microseconds * 3e6), transcendentals=0)


def lane_of(rows):
    return lax.broadcasted_iota(jnp.int32, (rows, LANES), 1)


def take(value, index):
    return jnp.take_along_axis(value, index, axis=1, mode="promise_in_bounds")


def near_edges(rows):
    k = lane_of(rows) % GROUP
    return jnp.where(k < HALO, HALO - 1 - k, LANES + HALO - 1 - k)


def far_edges(rows):
    k = lane_of(rows) % GROUP
    return jnp.where(k < HALO, LANES - 1 - k, GROUP - 1 - k)


def split(value):
    high = value.astype(jnp.bfloat16)
    low = (value - high.astype(jnp.float32)).astype(jnp.bfloat16)
    return high, low


def exact_dot(onehot, value):
    high, low = split(value)
    both = jnp.concatenate([high, low], axis=0)
    return jnp.dot(jnp.concatenate([onehot, onehot], axis=1), both, preferred_element_type=jnp.float32)


def coupling(coef, warmth):
    flow = coef * warmth
    second = coolant_gain * coef * coef
    return jnp.concatenate([coef, flow, second, flow - second * warmth], axis=1)


def flip(z, layers, i):
    return jnp.where(z == 0, i, layers - 1 - i)


def pack_kernel(u_ref, p_ref, c_ref, k_ref, f_ref, x_ref, *refs):
    own_ref, left_ref, right_ref, seg_ref = refs[3:7]
    sems = refs[-1]
    layers, rows, _ = u_ref.shape
    seg = f_ref.shape[1]
    z = lax.axis_index("gz")
    plane = layers * rows
    copies = []

    def fetch(src, at, n):
        copies.append(pltpu.make_async_copy(src, own_ref.at[pl.ds(at, n), :], sems.at[len(copies)]))
        copies[-1].start()

    for field, ref in enumerate((k_ref.at[0], k_ref.at[1], u_ref, p_ref, c_ref)):
        for i in range(layers):
            fetch(ref.at[flip(z, layers, i)], field * plane + i * rows, rows)
    fetch(x_ref.at[0], RAW * plane, seg)
    fetch(f_ref.at[0], RAW * plane + seg, seg)
    for table, place in zip(refs[:3], refs[7:10]):
        copies.append(pltpu.make_async_copy(table, place, sems.at[len(copies)]))
        copies[-1].start()
    for field in range(2):
        for i in range(layers):
            copies[field * layers + i].wait()
            here = pl.ds(field * plane + i * rows, rows)
            own_ref[here, :] = jnp.sqrt(own_ref[here, :])
    for copy in copies[2 * layers :]:
        copy.wait()
    chunk = rows // 4
    lane = lane_of(chunk)
    first = lane % GROUP < HALO
    near, far = near_edges(chunk), far_edges(chunk)
    for part in range(RAW):
        even = jnp.zeros((chunk, LANES), jnp.float32)
        odd = even
        for h in range(2):
            for i in range(layers):
                here = lane // GROUP == h * layers + i
                for side in range(2):
                    g = 2 * h + side
                    if part < 4:
                        at = g * plane + i * rows + part * chunk
                    else:
                        at = 4 * plane + i * rows + g * chunk
                    block = own_ref[at : at + chunk, :]
                    if side == 0:
                        even = jnp.where(here, take(block, near), even)
                    else:
                        odd = jnp.where(here, take(block, far), odd)
        left_ref[part * chunk : (part + 1) * chunk, :] = jnp.where(first, even, odd)
        right_ref[part * chunk : (part + 1) * chunk, :] = jnp.where(first, odd, even)
    segments = own_ref[RAW * plane : RAW * plane + 2 * seg, :]
    left_ref[RAW * chunk :, :] = segments
    right_ref[RAW * chunk :, :] = segments
    seg_ref[...] = segments


class Strips:
    def __init__(self, ref, right_at, left_at, rows, layers):
        self.ref, self.right_at, self.left_at = ref, right_at, left_at
        self.rows, self.layers = rows, layers

    def merged(self, field, start, n, x, gx):
        chunk = self.rows // 4
        if field < 4:
            g, at = field, start
        else:
            g, at = start // chunk, 4 * chunk + start % chunk
        ref_r, ref_l = self.ref
        a = ref_r[self.right_at + at : self.right_at + at + n, :]
        b = ref_l[self.left_at + at : self.left_at + at + n, :]
        a = jnp.where(x < gx - 1, a, 0.0)
        b = jnp.where(x > 0, b, 0.0)
        first = lane_of(n) % GROUP < HALO
        return g, (jnp.where(first, a, b) if g % 2 == 0 else jnp.where(first, b, a))

    def halo(self, field, start, n, x, gx, partner):
        g, both = self.merged(field, start, n, x, gx)
        lane = lane_of(n)
        half = self.layers * GROUP
        src = lane % half
        if partner:
            src = (self.layers - 1 - src // GROUP) * GROUP + src % GROUP
        if g % 2 == 1:
            src = jnp.where(src % GROUP < HALO, src + HALO, src - HALO)
        return take(both, src + half * (g // 2))


def place_segments(x, gx, seg, coef_ref, warmth_ref, first, rest):
    coef, warmth = first
    coef_ref[pl.ds(pl.multiple_of(x * seg, seg), seg), :] = coef
    warmth_ref[pl.ds(pl.multiple_of(x * seg, seg), seg), :] = warmth
    for k, (ref, at) in enumerate(rest, 1):
        holder = lax.rem(x + k, gx)
        place = pl.ds(pl.multiple_of(holder * seg, seg), seg)
        coef_ref[place, :] = ref[at : at + seg, :]
        warmth_ref[place, :] = ref[at + seg : at + 2 * seg, :]


def tables(z, group, layers, holder_ref, stratum_ref, transverse_ref):
    holder = holder_ref[pl.ds(group, 1), :]
    layer = stratum_ref[pl.ds(group, 1), :]
    layer = jnp.where(z == 0, layer, layers - 1 - layer)
    row = transverse_ref[pl.ds(group, 1), :]
    n = holder.shape[1]
    which = lax.broadcasted_iota(jnp.int32, (8, n), 0)
    stacked = jnp.where(which == 0, holder, jnp.where(which == 1, layer, row))
    eye = lax.broadcasted_iota(jnp.int32, (n, n), 0) == lax.broadcasted_iota(jnp.int32, (n, n), 1)
    columns = lax.dot_general(
        eye.astype(jnp.float32).astype(jnp.bfloat16),
        stacked.astype(jnp.float32).astype(jnp.bfloat16),
        (((1,), (1,)), ((), ())),
        preferred_element_type=jnp.float32,
    )
    return (holder, layer, row), columns


def as_onehot(mask):
    return jnp.where(mask, 1.0, 0.0).astype(jnp.bfloat16)


def halo_segments(coef, warmth, columns, base, x):
    n = coef.shape[0]
    lane = lane_of(n)
    holder, layer = columns[:, 0:1].astype(jnp.int32), columns[:, 1:2].astype(jnp.int32)
    side = jnp.where(lane % GROUP < HALO, x + 1, x - 1)
    mine = jnp.logical_and(lane // GROUP == layer + base, holder == side)
    near = near_edges(n)
    return coupling(jnp.where(mine, take(coef, near), 0.0), take(warmth, near))


def combine(raw, added):
    s, t, u, power, storage = raw
    wall, flow, second, later = (added[:, i * LANES : (i + 1) * LANES] for i in range(4))
    return s, t, s * u, storage + wall, power + storage * u + flow, power + later, storage + second


def starts_of(gx, chunk, seg):
    lengths = [RAW * chunk + 2 * seg if k in (1, gx - 1) else 2 * seg for k in range(1, gx)]
    return [sum(lengths[:k]) for k in range(gx)]


def edge_at(top, rows):
    return 0 if top is True else rows - HALO if top is False else pl.multiple_of(jnp.where(top, 0, rows - HALO), HALO)


def inner_at(top, rows):
    return HALO if top is True else rows - 2 * HALO if top is False else pl.multiple_of(jnp.where(top, HALO, rows - 2 * HALO), HALO)


def sides_of(gy, y):
    return [(y == 1, True)] if gy == 2 else [(True, y > 0), (False, y < gy - 1)]


def fill_kernel(partner, gx, gy, shape, seg, *refs):
    layers, rows = shape
    cells_ref, holder_ref, stratum_ref, transverse_ref = refs[:4]
    plane, chunk = layers * rows, rows // 4
    starts = starts_of(gx, chunk, seg)
    if partner:
        received = [refs[4]] * (gx - 1)
        refs = refs[5:]
    else:
        received = refs[4 : 4 + gx - 1]
        refs = refs[4 + gx - 1 :]
        starts = [0] * gx
    sides = 1 if gy == 2 else 2
    out_ref = refs[0]
    if partner:
        coef_ref, warmth_ref = refs[1:3]
    else:
        strip_refs, info_ref, segments_ref = refs[1 : 1 + sides], refs[1 + sides], refs[2 + sides]
        n = segments_ref.shape[0] // 2
        coef_ref, warmth_ref = segments_ref.at[pl.ds(0, n), :], segments_ref.at[pl.ds(n, n), :]
    x, y, z = (lax.axis_index(a) for a in ("gx", "gy", "gz"))
    base = layers if partner else 0
    rest = [(r, starts[k] + (RAW * chunk if k in (0, gx - 2) else 0)) for k, r in enumerate(received)]
    at = RAW * plane
    first = (cells_ref[at : at + seg, :], cells_ref[at + seg : at + 2 * seg, :])
    place_segments(x, gx, seg, coef_ref, warmth_ref, first, rest)
    group = y * 2 + ((1 - z) if partner else z)
    (holder, layer, row), columns = tables(z, group, layers, holder_ref, stratum_ref, transverse_ref)
    coef, warmth = coef_ref[...], warmth_ref[...]
    n = coef.shape[0]
    if not partner:
        info_ref[...] = columns

    cell = jnp.where(holder == x, layer * rows + row, -1)
    line = lax.broadcasted_iota(jnp.int32, (plane, n), 0)
    added = exact_dot(as_onehot(line == cell), coupling(coef, warmth))
    line = lax.broadcasted_iota(jnp.int32, (rows, n), 0)
    beside = exact_dot(as_onehot(line == row), halo_segments(coef, warmth, columns, base, x))
    for i in range(layers):
        src = layers - 1 - i if partner else i
        raw = [cells_ref[f * plane + src * rows : f * plane + (src + 1) * rows, :] for f in range(RAW)]
        for f, value in enumerate(combine(raw, added[i * rows : (i + 1) * rows])):
            out_ref[f * (layers + 1) + i] = value
    strips = Strips((received[0], received[-1]), starts[0], starts[gx - 2], rows, layers)
    half = lane_of(chunk) // (LANES // 2) == (1 if partner else 0)
    for part in range(4):
        here = slice(part * chunk, (part + 1) * chunk)
        raw = [jnp.where(half, strips.halo(f, part * chunk, chunk, x, gx, partner), 0.0) for f in range(RAW)]
        for f, value in enumerate(combine(raw, beside[here])):
            out_ref[f * (layers + 1) + layers, here, :] = value
    if partner:
        return
    low = lane_of(HALO) < LANES // 2
    for strip_ref, (top, _) in zip(strip_refs, sides_of(gy, y)):
        edge = pl.ds(edge_at(top, rows), HALO)
        for f in range(FIELDS):
            for i in range(layers):
                strip_ref[(f * layers + i) * HALO : (f * layers + i + 1) * HALO, :] = out_ref[f * (layers + 1) + i, edge, :]
        at = FIELDS * layers * HALO
        made = [out_ref[f * (layers + 1) + layers, edge, :] for f in range(FIELDS)]
        made.append(jnp.zeros_like(made[0]))
        for j in range(4):
            packed = jnp.where(low, made[2 * j], pltpu.roll(made[2 * j + 1], LANES // 2, 1))
            strip_ref[at + j * HALO : at + (j + 1) * HALO, :] = packed


def lateral(buf, at, n, count):
    lane = lane_of(n)
    k, group = lane % GROUP, lane // GROUP
    top = buf.shape[0] - 1
    centre = [buf[i, pl.ds(at, n), :] for i in range(min(count + 1, top))]
    halo = buf[top, pl.ds(at, n), :]
    border = jnp.zeros_like(halo)
    sums = []
    for i in range(count):
        border = jnp.where(group == i, pltpu.roll(centre[i], i * GROUP + HALO, 1), border)
        beside = pltpu.roll(halo, LANES - (i * GROUP + HALO), 1)
        east = jnp.where(lane == LANES - 1, beside, pltpu.roll(centre[i], LANES - 1, 1))
        west = jnp.where(lane == 0, beside, pltpu.roll(centre[i], 1, 1))
        sums.append(east + west + buf[i, pl.ds(at - 1, n), :] + buf[i, pl.ds(at + 1, n), :])
    one = jnp.where(k == HALO, border, pltpu.roll(halo, 1, 1))
    other = jnp.where(k == HALO - 1, border, pltpu.roll(halo, LANES - 1, 1))
    sums.append(one + other + buf[top, pl.ds(at - 1, n), :] + buf[top, pl.ds(at + 1, n), :])
    return centre + [halo], sums


def vertical(values, count):
    planes, halo = values[:-1], values[-1]
    sums = []
    for i in range(count):
        near = [planes[j] for j in (i - 1, i + 1) if 0 <= j < len(planes)]
        sums.append(functools.reduce(jnp.add, near))
    lane = lane_of(halo.shape[0])
    up = jnp.where(lane >= GROUP, pltpu.roll(halo, GROUP, 1), 0.0)
    down = jnp.where(lane < LANES - GROUP, pltpu.roll(halo, LANES - GROUP, 1), 0.0)
    sums.append(up + down)
    return sums


def coefficients(s_ref, at, n, raw, dests, to):
    a_ref, b_ref, q_ref, r_ref, e_ref, g_ref = dests
    top = s_ref.shape[0] - 1
    centre, sums = lateral(s_ref, at, n, top)
    t = [raw(1, i) for i in range(top + 1)]
    above = vertical(t, top)
    here = pl.ds(to, n)
    for i in range(top + 1):
        s = centre[i]
        diag = raw(3, i) + s * sums[i] + t[i] * above[i]
        inverse = 1.0 / jnp.where(diag > 0.0, diag, 1.0)
        scaled = s * inverse
        a_ref[i, here, :] = s * scaled
        b_ref[i, here, :] = t[i] * scaled
        r_ref[i, here, :] = raw(4, i) * scaled
        e_ref[i, here, :] = raw(5, i) * scaled
        g_ref[i, here, :] = raw(6, i) * inverse
        q_ref[i, here, :] = t[i] * jnp.where(s > 0.0, 1.0 / jnp.where(s > 0.0, s, 1.0), 0.0)


def sweep(src_ref, dst_ref, at, n, count, coefs, base):
    a_ref, b_ref, q_ref, r_ref = coefs[:4]
    top = src_ref.shape[0] - 1
    here = pl.ds(base, n)
    centre, sums = lateral(src_ref, at, n, count)
    layers = list(range(len(centre) - 1)) + [top]
    above = vertical([q_ref[i, here, :] * c for i, c in zip(layers, centre)], count)
    for j, i in enumerate(list(range(count)) + [top]):
        value = r_ref[i, here, :] + a_ref[i, here, :] * sums[j] + b_ref[i, here, :] * above[j]
        dst_ref[i, pl.ds(at, n), :] = value


def next_rhs(coefs, v_ref, at, n, base):
    r_ref, e_ref, g_ref = coefs[3:]
    here = pl.ds(base, n)
    for i in range(v_ref.shape[0]):
        r_ref[i, here, :] = e_ref[i, here, :] + g_ref[i, here, :] * v_ref[i, pl.ds(at, n), :]


def needed(layers, n):
    return min(2 * layers, layers + STEPS * ITERS - 1 - n)


def two_steps(layers, sweep_all, between, after):
    for step in range(STEPS):
        whole = [n for n in range(step * ITERS, (step + 1) * ITERS) if needed(layers, n) == 2 * layers]
        pairs = len(whole) // 2

        def pair(k, carry):
            n = step * ITERS + 2 * k
            sweep_all(n, 0, 2 * layers)
            sweep_all(n + 1, 1, 2 * layers)
            return carry

        if pairs:
            lax.fori_loop(0, pairs, pair, 0)
        for n in range(step * ITERS + 2 * pairs, (step + 1) * ITERS):
            sweep_all(n, n % 2, needed(layers, n))
        after(step)
        if step < STEPS - 1:
            between()


PAD = 8


def tile_kernel(gx, gy, shape, *refs):
    layers, rows = shape
    own_ref, partner_ref, info_ref, out_ref, below_ref, level_ref = refs[:6]
    s_ref, va_ref, vb_ref = refs[6:9]
    coefs = refs[9:]
    x, y, z = (lax.axis_index(a) for a in ("gx", "gy", "gz"))
    top = 2 * layers
    zeros = jnp.zeros((PAD, LANES), jnp.float32)
    for ref in (s_ref, va_ref, vb_ref):
        for i in range(top + 1):
            ref[i, 0:PAD, :] = zeros
            ref[i, PAD + rows : PAD + rows + PAD, :] = zeros

    def field(f, i, here):
        j = f * (layers + 1)
        if i == top:
            return own_ref[j + layers, here, :] + partner_ref[j + layers, here, :]
        return own_ref[j + i, here, :] if i < layers else partner_ref[j + i - layers, here, :]

    for i in range(top + 1):
        s_ref[i, PAD : PAD + rows, :] = field(0, i, slice(None))
        va_ref[i, PAD : PAD + rows, :] = field(2, i, slice(None))
    n = 16
    for at in range(0, rows, n):
        coefficients(s_ref, PAD + at, n, lambda f, i: field(f, i, slice(at, at + n)), coefs, at)

    bufs = (va_ref, vb_ref)
    sides = sides_of(gy, y)

    def sweep_all(number, which, count):
        src_ref, dst_ref = bufs[which], bufs[1 - which]
        for side, (above, _) in enumerate(sides):
            inner = pl.ds(PAD + inner_at(above, rows), HALO)
            for i in range(top + 1):
                level_ref[(side * STEPS * ITERS + number) * (top + 1) + i] = src_ref[i, inner, :]
        for at in range(0, rows, n):
            sweep(src_ref, dst_ref, PAD + at, n, count, coefs, at)

    holder, layer, row = (info_ref[:, j : j + 1].astype(jnp.int32) for j in range(3))
    spoilt = None
    for above, live in sides:
        part = jnp.logical_and(row // HALO == edge_at(above, rows) // HALO, live)
        spoilt = part if spoilt is None else jnp.logical_or(spoilt, part)
    cell = jnp.where(jnp.logical_and(holder == x, jnp.logical_not(spoilt)), layer * rows + row, -1)
    picks = as_onehot(lax.broadcasted_iota(jnp.int32, (cell.shape[0], layers * rows), 1) == cell)

    def after(step):
        heat = []
        for i in range(layers):
            here = pl.ds(PAD, rows)
            heat.append(va_ref[i, here, :] / s_ref[i, here, :])
            if step == STEPS - 1:
                out_ref[flip(z, layers, i)] = heat[-1]
        below_ref[step] = exact_dot(picks, jnp.concatenate(heat, axis=0))

    def between():
        for at in range(0, rows, n):
            next_rhs(coefs, va_ref, PAD + at, n, at)

    two_steps(layers, sweep_all, between, after)


def edge_kernel(gx, gy, shape, seg, *refs):
    layers, rows = shape
    own_ref, partner_ref, info_ref, segments_ref, below_ref, level_ref = refs[:6]
    sides_n = 1 if gy == 2 else 2
    along, across = refs[6 : 6 + sides_n], refs[6 + sides_n : 6 + 2 * sides_n]
    refs = refs[6 + 2 * sides_n :]
    heat_ref, returns = refs[0], refs[1 : 1 + gx]
    ret_ref, s_ref, va_ref, vb_ref = refs[1 + gx : 5 + gx]
    coefs = refs[5 + gx :]
    x, y, z = (lax.axis_index(a) for a in ("gx", "gy", "gz"))
    top = 2 * layers
    count = info_ref.shape[0]
    holder, layer, row = (info_ref[:, j : j + 1].astype(jnp.int32) for j in range(3))
    below = [below_ref[step] for step in range(STEPS)]
    lane = lane_of(HALO)
    low = lane < LANES // 2
    bufs = (va_ref, vb_ref)

    def tile(j):
        return pl.ds(j if isinstance(j, int) else pl.multiple_of(j, HALO), HALO)

    for side, (above, live) in enumerate(sides_of(gy, y)):
        def place(when_top, otherwise):
            if above is True or above is False:
                return when_top * HALO if above else otherwise * HALO
            return jnp.where(above, when_top * HALO, otherwise * HALO)

        outer, strip, edge, inner = place(0, 3), place(1, 2), place(2, 1), place(3, 0)
        edge_rows = tile(edge_at(above, rows))
        inner_rows = tile(inner_at(above, rows))

        def field(f, i, here):
            j = f * (layers + 1)
            if i == top:
                return own_ref[j + layers, here, :] + partner_ref[j + layers, here, :]
            return own_ref[j + i, here, :] if i < layers else partner_ref[j + i - layers, here, :]

        t_ref, d_ref, q_ref, e_ref, g_ref = coefs[1], coefs[0], coefs[3], coefs[4], coefs[5]
        keep = {0: s_ref, 1: t_ref, 2: va_ref, 3: d_ref, 4: q_ref, 5: e_ref, 6: g_ref}
        zeros = jnp.zeros((HALO, LANES), jnp.float32)
        src = lane % (LANES // 2)
        turned = (layers - 1 - src // GROUP) * GROUP + src % GROUP
        for f in range(FIELDS):
            for i in range(top + 1):
                if i < top:
                    ref, j = (along[side], i) if i < layers else (across[side], top - 1 - i)
                    at = (f * layers + j) * HALO
                    value = ref[at : at + HALO, :]
                else:
                    at = FIELDS * layers * HALO + (f // 2) * HALO
                    half = (LANES // 2) * (f % 2)
                    a = take(along[side][at : at + HALO, :], src + half)
                    b = take(across[side][at : at + HALO, :], turned + half)
                    value = jnp.where(low, a, b)
                ref, shift = keep[f], 0 if f in (0, 2) else HALO
                ref[i, tile(strip - shift), :] = value
                ref[i, tile(edge - shift), :] = field(f, i, edge_rows)
        for i in range(top + 1):
            s_ref[i, tile(outer), :] = zeros
            va_ref[i, tile(outer), :] = zeros
            vb_ref[i, tile(outer), :] = zeros
            s_ref[i, tile(inner), :] = field(0, i, inner_rows)
        n = 2 * HALO
        held = [[keep[f][i, pl.ds(0, n), :] for i in range(top + 1)] if f in (1, 3, 4, 5, 6) else None for f in range(FIELDS)]
        coefficients(s_ref, HALO, n, lambda f, i: held[f][i], coefs, 0)

        def sweep_all(number, which, needed_layers):
            src_ref, dst_ref = bufs[which], bufs[1 - which]
            for i in range(top + 1):
                src_ref[i, tile(inner), :] = level_ref[(side * STEPS * ITERS + number) * (top + 1) + i]
            sweep(src_ref, dst_ref, HALO, n, needed_layers, coefs, 0)

        first = edge_at(above, rows)
        hit = jnp.logical_and(jnp.logical_and(holder == x, row // HALO == first // HALO), live)
        cell = jnp.where(hit, layer * HALO + row - first, -1)
        picks = as_onehot(lax.broadcasted_iota(jnp.int32, (count, LANES), 1) == cell)

        def after(step):
            heat = []
            for i in range(layers):
                heat.append(va_ref[i, tile(edge), :] / s_ref[i, tile(edge), :])
                if step == STEPS - 1:
                    heat_ref[side * layers + flip(z, layers, i)] = heat[-1]
            heat.append(jnp.zeros((LANES - layers * HALO, LANES), jnp.float32))
            below[step] = below[step] + exact_dot(picks, jnp.concatenate(heat, axis=0))

        two_steps(layers, sweep_all, lambda: next_rhs(coefs, va_ref, HALO, n, 0), after)

    coef, warmth = segments_ref[:count, :], segments_ref[count:, :]
    for step in range(STEPS):
        warmth = warmth + coolant_gain * coef * (below[step] - warmth)
    ret_ref[...] = jnp.where(holder == x, warmth, 0.0)
    for k, ref in enumerate(returns):
        owner = lax.rem(x + k, gx)
        ref[...] = ret_ref[pl.ds(pl.multiple_of(owner * seg, seg), seg), :]


def merge_kernel(gy, whole_ref, heat_ref, out_ref):
    layers, rows, _ = whole_ref.shape
    out_ref[...] = whole_ref[...]
    for side, (above, live) in enumerate(sides_of(gy, lax.axis_index("gy"))):
        def put(side=side, above=above):
            out_ref[:, pl.ds(edge_at(above, rows), HALO), :] = heat_ref[side * layers : (side + 1) * layers]

        if live is True:
            put()
        else:
            pl.when(live)(put)


def local(gx, gy, gz, u, power, storage, conductance, warmth, coef, holder, stratum, transverse):
    layers, rows, columns = u.shape
    seg = warmth.shape[1]
    segments = stratum.shape[1]
    if gz != 2 or gx < 3 or columns != LANES or 2 * layers * GROUP != LANES or rows % 32:
        raise ValueError("unsupported shape")
    holder = holder[:, :, 0]
    shape = (layers, rows)
    f32 = jnp.float32
    chunk = rows // 4
    wide = RAW * chunk + 2 * seg

    def struct(*dims):
        return jax.ShapeDtypeStruct(dims, f32)

    def vmem(*dims):
        return pltpu.VMEM(dims, f32)

    indices = (holder, stratum, transverse)
    own, to_left, to_right, only, *indices = pl.pallas_call(
        pack_kernel,
        out_shape=(
            struct(RAW * layers * rows + 2 * seg, LANES),
            struct(wide, LANES),
            struct(wide, LANES),
            struct(2 * seg, LANES),
            *(jax.ShapeDtypeStruct(a.shape, a.dtype) for a in indices),
        ),
        in_specs=[pl.BlockSpec(memory_space=pltpu.HBM)] * 9,
        out_specs=(VMEM,) * 7,
        scratch_shapes=[pltpu.SemaphoreType.DMA((RAW * layers + 5,))],
        compiler_params=PARAMS,
        name="pack",
    )(*(pltpu.with_memory_space_constraint(a, pltpu.HBM) for a in (u, power, storage, conductance, warmth, coef, *indices)))

    swap = [(0, 1), (1, 0)]
    partner = lax.ppermute(own, "gz", swap)
    received = []
    for k in range(1, gx):
        payload = to_left if k == 1 else to_right if k == gx - 1 else only
        received.append(lax.ppermute(payload, "gx", [(i, (i - k) % gx) for i in range(gx)]))
    late = lax.ppermute(jnp.concatenate(received, axis=0), "gz", swap)

    sides = 1 if gy == 2 else 2
    fields = struct(FIELDS * (layers + 1), rows, LANES)
    strip_rows = FIELDS * layers * HALO + 4 * HALO
    filled = pl.pallas_call(
        functools.partial(fill_kernel, False, gx, gy, shape, seg),
        out_shape=(fields,) + (struct(strip_rows, LANES),) * sides + (struct(segments, 8), struct(2 * segments, LANES)),
        in_specs=[VMEM] * (4 + gx - 1),
        out_specs=(VMEM,) * (3 + sides),
        compiler_params=PARAMS,
        cost_estimate=cost(1.5),
        name="fill_own",
    )(own, *indices, *received)
    own_fields, strips, (info, held) = filled[0], filled[1 : 1 + sides], filled[1 + sides :]
    if gy == 2:
        routes = [(strips[0], swap)]
    else:
        up = [(i, i + 1) for i in range(gy - 1)]
        routes = [(strips[1], up), (strips[0], [(j, i) for i, j in up])]
    along = [lax.ppermute(value, "gy", pairs) for value, pairs in routes]
    across = []
    for value, pairs in routes:
        both = [(2 * i + z, 2 * j + 1 - z) for i, j in pairs for z in range(2)]
        across.append(lax.ppermute(value, ("gy", "gz"), both))

    partner_fields = pl.pallas_call(
        functools.partial(fill_kernel, True, gx, gy, shape, seg),
        out_shape=fields,
        in_specs=[VMEM] * 5,
        out_specs=VMEM,
        scratch_shapes=[vmem(segments, LANES)] * 2,
        compiler_params=PARAMS,
        cost_estimate=cost(1.5),
        name="fill_partner",
    )(partner, *indices, late)

    top = 2 * layers
    padded = vmem(top + 1, rows + 2 * PAD, LANES)
    inside, below, levels = pl.pallas_call(
        functools.partial(tile_kernel, gx, gy, shape),
        out_shape=(
            struct(layers, rows, LANES),
            struct(STEPS, segments, LANES),
            struct(sides * STEPS * ITERS * (top + 1), HALO, LANES),
        ),
        in_specs=[VMEM] * 3,
        out_specs=(VMEM,) * 3,
        scratch_shapes=[padded] * 3 + [vmem(top + 1, rows, LANES)] * 6,
        compiler_params=PARAMS,
        cost_estimate=cost(7),
        name="tile_sweeps",
    )(own_fields, partner_fields, info)

    results = pl.pallas_call(
        functools.partial(edge_kernel, gx, gy, shape, seg),
        out_shape=(struct(sides * layers, HALO, LANES),) + (struct(seg, LANES),) * gx,
        in_specs=[VMEM] * (6 + 2 * sides),
        out_specs=(VMEM,) * (1 + gx),
        scratch_shapes=[vmem(segments, LANES)]
        + [vmem(top + 1, 4 * HALO, LANES)] * 3
        + [vmem(top + 1, 2 * HALO, LANES)] * 6,
        compiler_params=PARAMS,
        cost_estimate=cost(1.5),
        name="edge_sweeps",
    )(own_fields, partner_fields, info, held, below, levels, *along, *across)
    heat, total = results[0], results[1]
    returned = [lax.ppermute(results[1 + k], "gx", [(i, (i + k) % gx) for i in range(gx)]) for k in range(1, gx)]
    temperature = pl.pallas_call(
        functools.partial(merge_kernel, gy),
        out_shape=struct(layers, rows, LANES),
        in_specs=[VMEM] * 2,
        out_specs=VMEM,
        compiler_params=PARAMS,
        cost_estimate=cost(1),
        name="merge",
    )(inside, heat)
    for value in returned:
        total = total + value
    return temperature, total[None]


def solution(mesh):
    gx, gy, gz = (mesh.shape[a] for a in ("gx", "gy", "gz"))
    cells = P(("stack", "gz"), "gy", "gx")
    segments = P(("stack", "gy", "gz"), "gx", None)
    return jax.shard_map(
        functools.partial(local, gx, gy, gz),
        mesh=mesh,
        in_specs=(cells, cells, cells, P(None, ("stack", "gz"), "gy", "gx"), segments, segments, P(), P(), P()),
        out_specs=(cells, segments),
        check_vma=False,
    )
```

profile of v0, /device:TPU:0, one launch (start us, length us, event | category | flops | bytes accessed | tf_op | source)
XLA Modules:
  0.0 33.7 jit_solution(17990975241503363553)
XLA Ops:
  0.6 2.2 %pack.1 = (f32[2624,128]{1,0:T(8,128)S(1)}, f32[224,128]{1,0:T(8,128)S(1)}, f32[224,128]{1,0:T(8,128)S(1)}, f32[64,128]{1,0:T(8,128)S(1)}, s32[4,128]{1,0:T(4,12...) custom-call(f32[4,128,128]{2,1,0:T(8,128)} %u_ref.1, f32[4,128,128]{2,1,0:T(8,128)} %p_ref.1, f32[4,128,128]{2,1,0:T(8,128)} %c_ref.1, ...), custom_call_target="tpu_custom_call" | custom-call | tf_op jit(solution)/shard_map/pack/pallas_call | solution.py:577
  2.9 0.5 %collective-permute-start.3 = (f32[2624,128]{1,0:T(8,128)S(1)}, f32[2624,128]{1,0:T(8,128)S(1)}, u32[]{:S(2)}, u32[]{:S(2)}) collective-permute-start(f32[2624,128]{1,0:T(8,128)S(1)} %get-tuple-element.21.refs_0_), channel_id=1, source_target_pairs={{0,1},{1,0},{2,3},{3,2},{4,5},{5,4},{6,7},{7,6},{8,9},{9,8},{10,11... | collective-permute-start | bytes 4030472 | tf_op jit(solution)/shard_map/ppermute | solution.py:594
  3.4 4.7 %collective-permute-start = (f32[224,128]{1,0:T(8,128)S(1)}, f32[224,128]{1,0:T(8,128)S(1)}, u32[]{:S(2)}, u32[]{:S(2)}) collective-permute-start(f32[224,128]{1,0:T(8,128)S(1)} %get-tuple-element.25), channel_id=1, source_target_pairs={{0,12},{4,0},{8,4},{12,8},{1,13},{5,1},{9,5},{13,9},{2,14},{6,2},{... | collective-permute-start | bytes 344072 | tf_op jit(solution)/shard_map/ppermute | solution.py:598
  8.0 0.0 collective-permute-start.2
  8.0 1.0 %collective-permute-start.1 = (f32[64,128]{1,0:T(8,128)S(1)}, f32[64,128]{1,0:T(8,128)S(1)}, u32[]{:S(2)}, u32[]{:S(2)}) collective-permute-start(f32[64,128]{1,0:T(8,128)S(1)} %get-tuple-element.26), channel_id=1, source_target_pairs={{0,8},{4,12},{8,0},{12,4},{1,9},{5,13},{9,1},{13,5},{2,10},{6,14},... | collective-permute-start | bytes 98312 | tf_op jit(solution)/shard_map/ppermute | solution.py:598
  9.1 7.0 %collective-permute-done.1.refs_5_ = f32[64,128]{1,0:T(8,128)S(1)} collective-permute-done((f32[64,128]{1,0:T(8,128)S(1)}, f32[64,128]{1,0:T(8,128)S(1)}, u32[]{:S(2)}, u32[]{:S(2)}) %collective-permute-start.1) | collective-permute-done | bytes 32800 | tf_op jit(solution)/shard_map/ppermute | solution.py:598
  16.0 0.0 collective-permute-done.refs_4_
  16.0 0.0 collective-permute-done.2.refs_6_
  16.0 0.1 collective-permute-start.4
  16.1 0.7 %fill_own.1 = (f32[35,128,128]{2,1,0:T(8,128)S(1)}, f32[256,128]{1,0:T(8,128)S(1)}, f32[128,8]{1,0:T(8,128)S(1)}, f32[256,128]{1,0:T(8,128)S(1)}) custom-call(f32[2624,128]{1,0:T(8,128)S(1)} %get-tuple-element.21.refs_0_, s32[4,128]{1,0:T(4,128)S(1)} %get-tuple-element.22.refs_1_, s32[4,128]{1,0:T(4,128)S(1)} %get-tuple-element.23.refs_2_, ...), custom_call_target="tpu_custom_call" | custom-call | bytes 4500000 | tf_op jit(solution)/shard_map/fill_own/pallas_call | solution.py:604
  16.8 1.6 %collective-permute-start.6 = (f32[256,128]{1,0:T(8,128)S(1)}, f32[256,128]{1,0:T(8,128)S(1)}, u32[]{:S(2)}, u32[]{:S(2)}) collective-permute-start(f32[256,128]{1,0:T(8,128)S(1)} %get-tuple-element.34), channel_id=1, source_target_pairs={{0,3},{1,2},{2,1},{3,0},{4,7},{5,6},{6,5},{7,4},{8,11},{9,10},{10,... | collective-permute-start | bytes 393224 | tf_op jit(solution)/shard_map/ppermute | solution.py:623
  18.4 0.5 %collective-permute-start.5 = (f32[256,128]{1,0:T(8,128)S(1)}, f32[256,128]{1,0:T(8,128)S(1)}, u32[]{:S(2)}, u32[]{:S(2)}) collective-permute-start(f32[256,128]{1,0:T(8,128)S(1)} %get-tuple-element.34), channel_id=1, source_target_pairs={{0,2},{2,0},{1,3},{3,1},{4,6},{6,4},{5,7},{7,5},{8,10},{10,8},{9,1... | collective-permute-start | bytes 393224 | tf_op jit(solution)/shard_map/ppermute | solution.py:619
  18.9 0.0 collective-permute-done.4.refs_4_
  18.9 0.5 %fill_partner.1.refs_1_ = f32[35,128,128]{2,1,0:T(8,128)S(1)} custom-call(f32[2624,128]{1,0:T(8,128)S(1)} %collective-permute-done.3.refs_0_, s32[4,128]{1,0:T(4,128)S(1)} %get-tuple-element.22.refs_1_, s32[4,128]{1,0:T(4,128)S(1)} %get-tuple-element.23.refs_2_, s32[4,128]{1,0:T(4,128)S(1)} %get-tuple-element.24.refs_3_, ...), custom_call_target="tpu_custom_call" | custom-call | bytes 4500000 | tf_op jit(solution)/shard_map/fill_partner/pallas_call | solution.py:625
  19.4 5.4 %tile_sweeps.1 = (f32[4,128,128]{2,1,0:T(8,128)S(1)}, f32[2,128,128]{2,1,0:T(8,128)S(1)}, f32[72,8,128]{2,1,0:T(8,128)S(1)}) custom-call(f32[35,128,128]{2,1,0:T(8,128)S(1)} %get-tuple-element.28.refs_0_, f32[35,128,128]{2,1,0:T(8,128)S(1)} %fill_partner.1.refs_1_, f32[128,8]{1,0:T(8,128)S(1)} %get-tuple-element.29.refs_2_), custom_call_target="tpu_custom_call" | custom-call | bytes 21000000 | tf_op jit(solution)/shard_map/tile_sweeps/pallas_call | solution.py:638
  24.9 0.6 %collective-permute-done.5.refs_6_ = f32[256,128]{1,0:T(8,128)S(1)} collective-permute-done((f32[256,128]{1,0:T(8,128)S(1)}, f32[256,128]{1,0:T(8,128)S(1)}, u32[]{:S(2)}, u32[]{:S(2)}) %collective-permute-start.5) | collective-permute-done | bytes 131104 | tf_op jit(solution)/shard_map/ppermute | solution.py:619
  25.4 1.5 %edge_sweeps.1 = (f32[4,8,128]{2,1,0:T(8,128)S(1)}, f32[32,128]{1,0:T(8,128)S(1)}, f32[32,128]{1,0:T(8,128)S(1)}, f32[32,128]{1,0:T(8,128)S(1)}, f32[32,128]{1,0:T(8,128)S(1)}) custom-call(f32[35,128,128]{2,1,0:T(8,128)S(1)} %get-tuple-element.28.refs_0_, f32[35,128,128]{2,1,0:T(8,128)S(1)} %fill_partner.1.refs_1_, f32[128,8]{1,0:T(8,128)S(1)} %get-tuple-element.29.refs_2_, ...), custom_call_target="tpu_custom_call" | custom-call | bytes 4500000 | tf_op jit(solution)/shard_map/edge_sweeps/pallas_call | solution.py:653
  27.0 0.5 %collective-permute-start.7 = (f32[32,128]{1,0:T(8,128)S(1)}, f32[32,128]{1,0:T(8,128)S(1)}, u32[]{:S(2)}, u32[]{:S(2)}) collective-permute-start(f32[32,128]{1,0:T(8,128)S(1)} %get-tuple-element.37), channel_id=1, source_target_pairs={{0,4},{4,8},{8,12},{12,0},{1,5},{5,9},{9,13},{13,1},{2,6},{6,10},{... | collective-permute-start | bytes 49160 | tf_op jit(solution)/shard_map/ppermute | solution.py:666
  27.4 1.3 %collective-permute-start.8 = (f32[32,128]{1,0:T(8,128)S(1)}, f32[32,128]{1,0:T(8,128)S(1)}, u32[]{:S(2)}, u32[]{:S(2)}) collective-permute-start(f32[32,128]{1,0:T(8,128)S(1)} %get-tuple-element.38), channel_id=1, source_target_pairs={{0,8},{4,12},{8,0},{12,4},{1,9},{5,13},{9,1},{13,5},{2,10},{6,14},... | collective-permute-start | bytes 49160 | tf_op jit(solution)/shard_map/ppermute | solution.py:666
  28.7 2.8 %collective-permute-start.9 = (f32[32,128]{1,0:T(8,128)S(1)}, f32[32,128]{1,0:T(8,128)S(1)}, u32[]{:S(2)}, u32[]{:S(2)}) collective-permute-start(f32[32,128]{1,0:T(8,128)S(1)} %get-tuple-element.39), channel_id=1, source_target_pairs={{0,12},{4,0},{8,4},{12,8},{1,13},{5,1},{9,5},{13,9},{2,14},{6,2},{... | collective-permute-start | bytes 49160 | tf_op jit(solution)/shard_map/ppermute | solution.py:666
  31.6 0.7 %merge.1 = f32[4,128,128]{2,1,0:T(8,128)} custom-call(f32[4,128,128]{2,1,0:T(8,128)S(1)} %get-tuple-element.30.whole_ref, f32[4,8,128]{2,1,0:T(8,128)S(1)} %get-tuple-element.35.heat_ref), custom_call_target="tpu_custom_call" | custom-call | bytes 3000000 | tf_op jit(solution)/shard_map/merge/pallas_call | solution.py:667
  32.3 0.4 %collective-permute-done.7 = f32[32,128]{1,0:T(8,128)S(1)} collective-permute-done((f32[32,128]{1,0:T(8,128)S(1)}, f32[32,128]{1,0:T(8,128)S(1)}, u32[]{:S(2)}, u32[]{:S(2)}) %collective-permute-start.7) | collective-permute-done | bytes 16416 | tf_op jit(solution)/shard_map/ppermute | solution.py:666
  32.7 0.5 %collective-permute-done.9 = f32[32,128]{1,0:T(8,128)S(1)} collective-permute-done((f32[32,128]{1,0:T(8,128)S(1)}, f32[32,128]{1,0:T(8,128)S(1)}, u32[]{:S(2)}, u32[]{:S(2)}) %collective-permute-start.9) | collective-permute-done | bytes 16416 | tf_op jit(solution)/shard_map/ppermute | solution.py:666
  33.1 0.6 %add_bitcast_fusion = f32[1,32,128]{2,1,0:T(8,128)} fusion(f32[32,128]{1,0:T(8,128)S(1)} %collective-permute-done.9, f32[32,128]{1,0:T(8,128)S(1)} %collective-permute-done.8, f32[32,128]{1,0:T(8,128)S(1)} %get-tuple-element.36, f32[32,128]{1,0:T(8,128)S(1)} %collective-permute-done.7), kind=kLoop, calls=%fused_computation.1 | loop fusion | flops 12288 | bytes 81920 | tf_op jit(solution)/shard_map/broadcast_in_dim | solution.py:678
  (4 shorter events, 0.0 us)
Async XLA Ops:
  2.9 16.1 %collective-permute-start.3 = (f32[2624,128]{1,0:T(8,128)S(1)}, f32[2624,128]{1,0:T(8,128)S(1)}, u32[]{:S(2)}, u32[]{:S(2)}) collective-permute-start(f32[2624,128]{1,0:T(8,128)S(1)} %get-tuple-element.21.refs_0_), channel_id=1, source_target_pairs={{0,1},{1,0},{2,3},{3,2},{4,5},{5,4},{6,7},{7,6},{8,9},{9,8},{10,11... | collective-permute-start | bytes 4030472 | tf_op jit(solution)/shard_map/ppermute | solution.py:594
  3.4 12.6 %collective-permute-start = (f32[224,128]{1,0:T(8,128)S(1)}, f32[224,128]{1,0:T(8,128)S(1)}, u32[]{:S(2)}, u32[]{:S(2)}) collective-permute-start(f32[224,128]{1,0:T(8,128)S(1)} %get-tuple-element.25), channel_id=1, source_target_pairs={{0,12},{4,0},{8,4},{12,8},{1,13},{5,1},{9,5},{13,9},{2,14},{6,2},{... | collective-permute-start | bytes 344072 | tf_op jit(solution)/shard_map/ppermute | solution.py:598
  8.0 8.0 %collective-permute-start.2 = (f32[224,128]{1,0:T(8,128)S(1)}, f32[224,128]{1,0:T(8,128)S(1)}, u32[]{:S(2)}, u32[]{:S(2)}) collective-permute-start(f32[224,128]{1,0:T(8,128)S(1)} %get-tuple-element.27), channel_id=1, source_target_pairs={{0,4},{4,8},{8,12},{12,0},{1,5},{5,9},{9,13},{13,1},{2,6},{6,10},{... | collective-permute-start | bytes 344072 | tf_op jit(solution)/shard_map/ppermute | solution.py:598
  8.0 8.0 %collective-permute-start.1 = (f32[64,128]{1,0:T(8,128)S(1)}, f32[64,128]{1,0:T(8,128)S(1)}, u32[]{:S(2)}, u32[]{:S(2)}) collective-permute-start(f32[64,128]{1,0:T(8,128)S(1)} %get-tuple-element.26), channel_id=1, source_target_pairs={{0,8},{4,12},{8,0},{12,4},{1,9},{5,13},{9,1},{13,5},{2,10},{6,14},... | collective-permute-start | bytes 98312 | tf_op jit(solution)/shard_map/ppermute | solution.py:598
  16.0 2.9 %collective-permute-start.4 = (f32[512,128]{1,0:T(8,128)S(1)}, f32[512,128]{1,0:T(8,128)S(1)}, u32[]{:S(2)}, u32[]{:S(2)}) collective-permute-start(f32[512,128]{1,0:T(8,128)S(1)} %pad_maximum_fusion), channel_id=1, source_target_pairs={{0,1},{1,0},{2,3},{3,2},{4,5},{5,4},{6,7},{7,6},{8,9},{9,8},{10,11... | collective-permute-start | bytes 786440 | tf_op jit(solution)/shard_map/ppermute | solution.py:599
  16.8 8.1 %collective-permute-start.6 = (f32[256,128]{1,0:T(8,128)S(1)}, f32[256,128]{1,0:T(8,128)S(1)}, u32[]{:S(2)}, u32[]{:S(2)}) collective-permute-start(f32[256,128]{1,0:T(8,128)S(1)} %get-tuple-element.34), channel_id=1, source_target_pairs={{0,3},{1,2},{2,1},{3,0},{4,7},{5,6},{6,5},{7,4},{8,11},{9,10},{10,... | collective-permute-start | bytes 393224 | tf_op jit(solution)/shard_map/ppermute | solution.py:623
  18.4 7.0 %collective-permute-start.5 = (f32[256,128]{1,0:T(8,128)S(1)}, f32[256,128]{1,0:T(8,128)S(1)}, u32[]{:S(2)}, u32[]{:S(2)}) collective-permute-start(f32[256,128]{1,0:T(8,128)S(1)} %get-tuple-element.34), channel_id=1, source_target_pairs={{0,2},{2,0},{1,3},{3,1},{4,6},{6,4},{5,7},{7,5},{8,10},{10,8},{9,1... | collective-permute-start | bytes 393224 | tf_op jit(solution)/shard_map/ppermute | solution.py:619
  27.0 5.7 %collective-permute-start.7 = (f32[32,128]{1,0:T(8,128)S(1)}, f32[32,128]{1,0:T(8,128)S(1)}, u32[]{:S(2)}, u32[]{:S(2)}) collective-permute-start(f32[32,128]{1,0:T(8,128)S(1)} %get-tuple-element.37), channel_id=1, source_target_pairs={{0,4},{4,8},{8,12},{12,0},{1,5},{5,9},{9,13},{13,1},{2,6},{6,10},{... | collective-permute-start | bytes 49160 | tf_op jit(solution)/shard_map/ppermute | solution.py:666
  27.4 5.2 %collective-permute-start.8 = (f32[32,128]{1,0:T(8,128)S(1)}, f32[32,128]{1,0:T(8,128)S(1)}, u32[]{:S(2)}, u32[]{:S(2)}) collective-permute-start(f32[32,128]{1,0:T(8,128)S(1)} %get-tuple-element.38), channel_id=1, source_target_pairs={{0,8},{4,12},{8,0},{12,4},{1,9},{5,13},{9,1},{13,5},{2,10},{6,14},... | collective-permute-start | bytes 49160 | tf_op jit(solution)/shard_map/ppermute | solution.py:666
  28.7 4.4 %collective-permute-start.9 = (f32[32,128]{1,0:T(8,128)S(1)}, f32[32,128]{1,0:T(8,128)S(1)}, u32[]{:S(2)}, u32[]{:S(2)}) collective-permute-start(f32[32,128]{1,0:T(8,128)S(1)} %get-tuple-element.39), channel_id=1, source_target_pairs={{0,12},{4,0},{8,4},{12,8},{1,13},{5,1},{9,5},{13,9},{2,14},{6,2},{... | collective-permute-start | bytes 49160 | tf_op jit(solution)/shard_map/ppermute | solution.py:666
where the time goes:
time: 33.9 us; the launch traced here: 33.7 us
  starting transfers between devices  13 us (38%)
  Pallas kernels  11 us (32%)
  waiting for transfers between devices  8.36 us (25%)
  between operations  0.69 us (2%)
  other arithmetic  0.63 us (2%)
    ppermute x3, waiting for transfers between devices, local(): lax.ppermute(payload, 'gx', [(i, (i - k) % gx) for i in range(gx)])  6.97 us
    ppermute x3, starting transfers between devices, local(): lax.ppermute(payload, 'gx', [(i, (i - k) % gx) for i in range(gx)])  5.68 us
    pallas_call x1, Pallas kernels, local(): pl.pallas_call(functools.partial(tile_kernel, gx, gy, shape), out_shape=(...  5.41 us
    ppermute x3, starting transfers between devices, local(): lax.ppermute(results[1 + k], 'gx', [(i, (i + k) % gx) for i in range(gx)])  4.6 us
    pallas_call x1, Pallas kernels, local(): pl.pallas_call(pack_kernel, out_shape=(struct(RAW * layers * rows + 2 * s...  2.22 us
    ppermute x1, starting transfers between devices, local(): across.append(lax.ppermute(value, ('gy', 'gz'), both))  1.6 us
    pallas_call x1, Pallas kernels, local(): pl.pallas_call(functools.partial(edge_kernel, gx, gy, shape, seg), out_sh...  1.54 us
    ppermute x3, waiting for transfers between devices, local(): lax.ppermute(results[1 + k], 'gx', [(i, (i + k) % gx) for i in range(gx)])  0.83 us
  transfers between devices with their start and end apart: 10, of which 4 were waited for; matrix products, arithmetic and copies ran while one was open for 0% of the time, Pallas kernels for 22%

commit v1 on v0

--- a/solution.py
+++ b/solution.py
@@ -64,37 +64,34 @@
     return jnp.where(z == 0, i, layers - 1 - i)
 
 
-def pack_kernel(u_ref, p_ref, c_ref, k_ref, f_ref, x_ref, *refs):
-    own_ref, left_ref, right_ref, seg_ref = refs[3:7]
+def pack_kernel(shape, u_ref, p_ref, c_ref, k_ref, f_ref, x_ref, *refs):
+    own_ref, even_ref, odd_ref, seg_ref = refs[3:7]
     sems = refs[-1]
-    layers, rows, _ = u_ref.shape
-    seg = f_ref.shape[1]
-    z = lax.axis_index("gz")
+    layers, rows = shape
+    seg = f_ref.shape[0]
+    x, z = lax.axis_index("gx"), lax.axis_index("gz")
     plane = layers * rows
     copies = []
 
-    def fetch(src, at, n):
-        copies.append(pltpu.make_async_copy(src, own_ref.at[pl.ds(at, n), :], sems.at[len(copies)]))
+    def fetch(src, dst):
+        copies.append(pltpu.make_async_copy(src, dst, sems.at[len(copies)]))
         copies[-1].start()
 
-    for field, ref in enumerate((k_ref.at[0], k_ref.at[1], u_ref, p_ref, c_ref)):
-        for i in range(layers):
-            fetch(ref.at[flip(z, layers, i)], field * plane + i * rows, rows)
-    fetch(x_ref.at[0], RAW * plane, seg)
-    fetch(f_ref.at[0], RAW * plane + seg, seg)
+    fetch(k_ref, own_ref.at[pl.ds(0, 2 * plane), :])
+    for field, ref in enumerate((u_ref, p_ref, c_ref), 2):
+        fetch(ref, own_ref.at[pl.ds(field * plane, plane), :])
+    for j, ref in enumerate((x_ref, f_ref)):
+        fetch(ref, own_ref.at[pl.ds(RAW * plane + j * seg, seg), :])
     for table, place in zip(refs[:3], refs[7:10]):
-        copies.append(pltpu.make_async_copy(table, place, sems.at[len(copies)]))
-        copies[-1].start()
-    for field in range(2):
-        for i in range(layers):
-            copies[field * layers + i].wait()
-            here = pl.ds(field * plane + i * rows, rows)
-            own_ref[here, :] = jnp.sqrt(own_ref[here, :])
-    for copy in copies[2 * layers :]:
+        fetch(table, place)
+    copies[0].wait()
+    roots = pl.ds(0, 2 * plane)
+    own_ref[roots, :] = jnp.sqrt(own_ref[roots, :])
+    for copy in copies[1:]:
         copy.wait()
     chunk = rows // 4
     lane = lane_of(chunk)
-    first = lane % GROUP < HALO
+    same = (lane % GROUP < HALO) == (x % 2 == 1)
     near, far = near_edges(chunk), far_edges(chunk)
     for part in range(RAW):
         even = jnp.zeros((chunk, LANES), jnp.float32)
@@ -102,46 +99,40 @@
         for h in range(2):
             for i in range(layers):
                 here = lane // GROUP == h * layers + i
+                src = flip(z, layers, i)
                 for side in range(2):
                     g = 2 * h + side
-                    if part < 4:
-                        at = g * plane + i * rows + part * chunk
-                    else:
-                        at = 4 * plane + i * rows + g * chunk
-                    block = own_ref[at : at + chunk, :]
+                    field, at = (g, part * chunk) if part < 4 else (4, g * chunk)
+                    block = own_ref[pl.ds(pl.multiple_of((field * layers + src) * rows + at, chunk), chunk), :]
                     if side == 0:
                         even = jnp.where(here, take(block, near), even)
                     else:
                         odd = jnp.where(here, take(block, far), odd)
-        left_ref[part * chunk : (part + 1) * chunk, :] = jnp.where(first, even, odd)
-        right_ref[part * chunk : (part + 1) * chunk, :] = jnp.where(first, odd, even)
+        even_ref[part * chunk : (part + 1) * chunk, :] = jnp.where(same, even, odd)
+        odd_ref[part * chunk : (part + 1) * chunk, :] = jnp.where(same, odd, even)
     segments = own_ref[RAW * plane : RAW * plane + 2 * seg, :]
-    left_ref[RAW * chunk :, :] = segments
-    right_ref[RAW * chunk :, :] = segments
     seg_ref[...] = segments
+    even_ref[RAW * chunk :, :] = segments
+    odd_ref[RAW * chunk :, :] = segments
 
 
 class Strips:
-    def __init__(self, ref, right_at, left_at, rows, layers):
-        self.ref, self.right_at, self.left_at = ref, right_at, left_at
+    def __init__(self, refs, starts, rows, layers):
+        self.refs, self.starts = refs, starts
         self.rows, self.layers = rows, layers
 
-    def merged(self, field, start, n, x, gx):
+    def merged(self, field, start, n, x):
         chunk = self.rows // 4
         if field < 4:
             g, at = field, start
         else:
             g, at = start // chunk, 4 * chunk + start % chunk
-        ref_r, ref_l = self.ref
-        a = ref_r[self.right_at + at : self.right_at + at + n, :]
-        b = ref_l[self.left_at + at : self.left_at + at + n, :]
-        a = jnp.where(x < gx - 1, a, 0.0)
-        b = jnp.where(x > 0, b, 0.0)
-        first = lane_of(n) % GROUP < HALO
-        return g, (jnp.where(first, a, b) if g % 2 == 0 else jnp.where(first, b, a))
-
-    def halo(self, field, start, n, x, gx, partner):
-        g, both = self.merged(field, start, n, x, gx)
+        a, b = (ref[at + begin : at + begin + n, :] for ref, begin in zip(self.refs, self.starts))
+        right_half = (lane_of(n) % GROUP < HALO) if g % 2 == 0 else (lane_of(n) % GROUP >= HALO)
+        return g, jnp.where(right_half == (x % 2 == 0), a, b)
+
+    def halo(self, field, start, n, x, partner):
+        g, both = self.merged(field, start, n, x)
         lane = lane_of(n)
         half = self.layers * GROUP
         src = lane % half
@@ -152,15 +143,19 @@
         return take(both, src + half * (g // 2))
 
 
-def place_segments(x, gx, seg, coef_ref, warmth_ref, first, rest):
-    coef, warmth = first
-    coef_ref[pl.ds(pl.multiple_of(x * seg, seg), seg), :] = coef
-    warmth_ref[pl.ds(pl.multiple_of(x * seg, seg), seg), :] = warmth
-    for k, (ref, at) in enumerate(rest, 1):
-        holder = lax.rem(x + k, gx)
+def place_segments(x, gx, seg, coef_ref, warmth_ref, own, even, odd, far):
+    def put(holder, source):
+        ref, at = source
         place = pl.ds(pl.multiple_of(holder * seg, seg), seg)
         coef_ref[place, :] = ref[at : at + seg, :]
         warmth_ref[place, :] = ref[at + seg : at + 2 * seg, :]
+
+    for k, source in far:
+        put(x ^ k, source)
+    put(x, own)
+    put(x ^ 1, even)
+    beside = jnp.where(x % 2 == 0, x - 1, x + 1)
+    pl.when(jnp.logical_and(beside >= 0, beside < gx))(lambda: put(beside, odd))
 
 
 def tables(z, group, layers, holder_ref, stratum_ref, transverse_ref):
@@ -201,9 +196,8 @@
     return s, t, s * u, storage + wall, power + storage * u + flow, power + later, storage + second
 
 
-def starts_of(gx, chunk, seg):
-    lengths = [RAW * chunk + 2 * seg if k in (1, gx - 1) else 2 * seg for k in range(1, gx)]
-    return [sum(lengths[:k]) for k in range(gx)]
+def lengths_of(gx, chunk, seg):
+    return [RAW * chunk + 2 * seg] * 2 + [2 * seg] * (gx - 2)
 
 
 def edge_at(top, rows):
@@ -222,14 +216,13 @@
     layers, rows = shape
     cells_ref, holder_ref, stratum_ref, transverse_ref = refs[:4]
     plane, chunk = layers * rows, rows // 4
-    starts = starts_of(gx, chunk, seg)
+    lengths = lengths_of(gx, chunk, seg)
     if partner:
-        received = [refs[4]] * (gx - 1)
+        sources = [(refs[4], sum(lengths[:k])) for k in range(gx)]
         refs = refs[5:]
     else:
-        received = refs[4 : 4 + gx - 1]
-        refs = refs[4 + gx - 1 :]
-        starts = [0] * gx
+        sources = [(ref, 0) for ref in refs[4 : 4 + gx]]
+        refs = refs[4 + gx :]
     sides = 1 if gy == 2 else 2
     out_ref = refs[0]
     if partner:
@@ -240,10 +233,8 @@
         coef_ref, warmth_ref = segments_ref.at[pl.ds(0, n), :], segments_ref.at[pl.ds(n, n), :]
     x, y, z = (lax.axis_index(a) for a in ("gx", "gy", "gz"))
     base = layers if partner else 0
-    rest = [(r, starts[k] + (RAW * chunk if k in (0, gx - 2) else 0)) for k, r in enumerate(received)]
-    at = RAW * plane
-    first = (cells_ref[at : at + seg, :], cells_ref[at + seg : at + 2 * seg, :])
-    place_segments(x, gx, seg, coef_ref, warmth_ref, first, rest)
+    even, odd = ((ref, at + RAW * chunk) for ref, at in sources[:2])
+    place_segments(x, gx, seg, coef_ref, warmth_ref, (cells_ref, RAW * plane), even, odd, list(enumerate(sources[2:gx], 2)))
     group = y * 2 + ((1 - z) if partner else z)
     (holder, layer, row), columns = tables(z, group, layers, holder_ref, stratum_ref, transverse_ref)
     coef, warmth = coef_ref[...], warmth_ref[...]
@@ -257,15 +248,15 @@
     line = lax.broadcasted_iota(jnp.int32, (rows, n), 0)
     beside = exact_dot(as_onehot(line == row), halo_segments(coef, warmth, columns, base, x))
     for i in range(layers):
-        src = layers - 1 - i if partner else i
-        raw = [cells_ref[f * plane + src * rows : f * plane + (src + 1) * rows, :] for f in range(RAW)]
+        src = flip(z, layers, i)
+        raw = [cells_ref[pl.ds(pl.multiple_of((f * layers + src) * rows, rows), rows), :] for f in range(RAW)]
         for f, value in enumerate(combine(raw, added[i * rows : (i + 1) * rows])):
             out_ref[f * (layers + 1) + i] = value
-    strips = Strips((received[0], received[-1]), starts[0], starts[gx - 2], rows, layers)
+    strips = Strips([ref for ref, _ in sources[:2]], [at for _, at in sources[:2]], rows, layers)
     half = lane_of(chunk) // (LANES // 2) == (1 if partner else 0)
     for part in range(4):
         here = slice(part * chunk, (part + 1) * chunk)
-        raw = [jnp.where(half, strips.halo(f, part * chunk, chunk, x, gx, partner), 0.0) for f in range(RAW)]
+        raw = [jnp.where(half, strips.halo(f, part * chunk, chunk, x, partner), 0.0) for f in range(RAW)]
         for f, value in enumerate(combine(raw, beside[here])):
             out_ref[f * (layers + 1) + layers, here, :] = value
     if partner:
@@ -318,7 +309,7 @@
 
 
 def coefficients(s_ref, at, n, raw, dests, to):
-    a_ref, b_ref, q_ref, r_ref, e_ref, g_ref = dests
+    a_ref, q_ref, r_ref, e_ref, g_ref = dests
     top = s_ref.shape[0] - 1
     centre, sums = lateral(s_ref, at, n, top)
     t = [raw(1, i) for i in range(top + 1)]
@@ -330,7 +321,6 @@
         inverse = 1.0 / jnp.where(diag > 0.0, diag, 1.0)
         scaled = s * inverse
         a_ref[i, here, :] = s * scaled
-        b_ref[i, here, :] = t[i] * scaled
         r_ref[i, here, :] = raw(4, i) * scaled
         e_ref[i, here, :] = raw(5, i) * scaled
         g_ref[i, here, :] = raw(6, i) * inverse
@@ -338,19 +328,21 @@
 
 
 def sweep(src_ref, dst_ref, at, n, count, coefs, base):
-    a_ref, b_ref, q_ref, r_ref = coefs[:4]
+    a_ref, q_ref, r_ref = coefs[:3]
     top = src_ref.shape[0] - 1
     here = pl.ds(base, n)
     centre, sums = lateral(src_ref, at, n, count)
     layers = list(range(len(centre) - 1)) + [top]
-    above = vertical([q_ref[i, here, :] * c for i, c in zip(layers, centre)], count)
+    ratio = [q_ref[i, here, :] for i in layers]
+    above = vertical([q * c for q, c in zip(ratio, centre)], count)
+    ratio = ratio[:count] + ratio[-1:]
     for j, i in enumerate(list(range(count)) + [top]):
-        value = r_ref[i, here, :] + a_ref[i, here, :] * sums[j] + b_ref[i, here, :] * above[j]
+        value = r_ref[i, here, :] + a_ref[i, here, :] * (sums[j] + ratio[j] * above[j])
         dst_ref[i, pl.ds(at, n), :] = value
 
 
 def next_rhs(coefs, v_ref, at, n, base):
-    r_ref, e_ref, g_ref = coefs[3:]
+    r_ref, e_ref, g_ref = coefs[2:]
     here = pl.ds(base, n)
     for i in range(v_ref.shape[0]):
         r_ref[i, here, :] = e_ref[i, here, :] + g_ref[i, here, :] * v_ref[i, pl.ds(at, n), :]
@@ -405,7 +397,7 @@
     for i in range(top + 1):
         s_ref[i, PAD : PAD + rows, :] = field(0, i, slice(None))
         va_ref[i, PAD : PAD + rows, :] = field(2, i, slice(None))
-    n = 16
+    n = 8
     for at in range(0, rows, n):
         coefficients(s_ref, PAD + at, n, lambda f, i: field(f, i, slice(at, at + n)), coefs, at)
 
@@ -482,7 +474,7 @@
                 return own_ref[j + layers, here, :] + partner_ref[j + layers, here, :]
             return own_ref[j + i, here, :] if i < layers else partner_ref[j + i - layers, here, :]
 
-        t_ref, d_ref, q_ref, e_ref, g_ref = coefs[1], coefs[0], coefs[3], coefs[4], coefs[5]
+        t_ref, d_ref, q_ref, e_ref, g_ref = coefs[1], coefs[0], coefs[2], coefs[3], coefs[4]
         keep = {0: s_ref, 1: t_ref, 2: va_ref, 3: d_ref, 4: q_ref, 5: e_ref, 6: g_ref}
         zeros = jnp.zeros((HALO, LANES), jnp.float32)
         src = lane % (LANES // 2)
@@ -538,8 +530,7 @@
         warmth = warmth + coolant_gain * coef * (below[step] - warmth)
     ret_ref[...] = jnp.where(holder == x, warmth, 0.0)
     for k, ref in enumerate(returns):
-        owner = lax.rem(x + k, gx)
-        ref[...] = ret_ref[pl.ds(pl.multiple_of(owner * seg, seg), seg), :]
+        ref[...] = ret_ref[pl.ds(pl.multiple_of((x ^ k) * seg, seg), seg), :]
 
 
 def merge_kernel(gy, whole_ref, heat_ref, out_ref):
@@ -559,7 +550,7 @@
     layers, rows, columns = u.shape
     seg = warmth.shape[1]
     segments = stratum.shape[1]
-    if gz != 2 or gx < 3 or columns != LANES or 2 * layers * GROUP != LANES or rows % 32:
+    if gz != 2 or gx < 4 or gx & (gx - 1) or columns != LANES or 2 * layers * GROUP != LANES or rows % 32:
         raise ValueError("unsupported shape")
     holder = holder[:, :, 0]
     shape = (layers, rows)
@@ -574,8 +565,9 @@
         return pltpu.VMEM(dims, f32)
 
     indices = (holder, stratum, transverse)
-    own, to_left, to_right, only, *indices = pl.pallas_call(
-        pack_kernel,
+    flat = [a.reshape(-1, LANES) for a in (u, power, storage, conductance, warmth, coef)]
+    own, to_even, to_odd, only, *indices = pl.pallas_call(
+        functools.partial(pack_kernel, shape),
         out_shape=(
             struct(RAW * layers * rows + 2 * seg, LANES),
             struct(wide, LANES),
@@ -585,17 +577,20 @@
         ),
         in_specs=[pl.BlockSpec(memory_space=pltpu.HBM)] * 9,
         out_specs=(VMEM,) * 7,
-        scratch_shapes=[pltpu.SemaphoreType.DMA((RAW * layers + 5,))],
+        scratch_shapes=[pltpu.SemaphoreType.DMA((9,))],
         compiler_params=PARAMS,
         name="pack",
-    )(*(pltpu.with_memory_space_constraint(a, pltpu.HBM) for a in (u, power, storage, conductance, warmth, coef, *indices)))
+    )(*(pltpu.with_memory_space_constraint(a, pltpu.HBM) for a in (*flat, *indices)))
 
     swap = [(0, 1), (1, 0)]
     partner = lax.ppermute(own, "gz", swap)
-    received = []
-    for k in range(1, gx):
-        payload = to_left if k == 1 else to_right if k == gx - 1 else only
-        received.append(lax.ppermute(payload, "gx", [(i, (i - k) % gx) for i in range(gx)]))
+    even = [(i, i ^ 1) for i in range(gx)]
+    odd = [pair for i in range(1, gx - 1, 2) for pair in ((i, i + 1), (i + 1, i))]
+    received = [lax.ppermute(to_even, "gx", even), lax.ppermute(to_odd, "gx", odd)]
+    far = {}
+    for k in range(2, gx):
+        far[k] = lax.ppermute(only, "gx", [(i, i ^ k) for i in range(gx) if abs(i - (i ^ k)) > 1])
+    received += [far[k] for k in range(2, gx)]
     late = lax.ppermute(jnp.concatenate(received, axis=0), "gz", swap)
 
     sides = 1 if gy == 2 else 2
@@ -604,7 +599,7 @@
     filled = pl.pallas_call(
         functools.partial(fill_kernel, False, gx, gy, shape, seg),
         out_shape=(fields,) + (struct(strip_rows, LANES),) * sides + (struct(segments, 8), struct(2 * segments, LANES)),
-        in_specs=[VMEM] * (4 + gx - 1),
+        in_specs=[VMEM] * (4 + gx),
         out_specs=(VMEM,) * (3 + sides),
         compiler_params=PARAMS,
         cost_estimate=cost(1.5),
@@ -644,7 +639,7 @@
         ),
         in_specs=[VMEM] * 3,
         out_specs=(VMEM,) * 3,
-        scratch_shapes=[padded] * 3 + [vmem(top + 1, rows, LANES)] * 6,
+        scratch_shapes=[padded] * 3 + [vmem(top + 1, rows, LANES)] * 5,
         compiler_params=PARAMS,
         cost_estimate=cost(7),
         name="tile_sweeps",
@@ -657,13 +652,13 @@
         out_specs=(VMEM,) * (1 + gx),
         scratch_shapes=[vmem(segments, LANES)]
         + [vmem(top + 1, 4 * HALO, LANES)] * 3
-        + [vmem(top + 1, 2 * HALO, LANES)] * 6,
+        + [vmem(top + 1, 2 * HALO, LANES)] * 5,
         compiler_params=PARAMS,
         cost_estimate=cost(1.5),
         name="edge_sweeps",
     )(own_fields, partner_fields, info, held, below, levels, *along, *across)
     heat, total = results[0], results[1]
-    returned = [lax.ppermute(results[1 + k], "gx", [(i, (i + k) % gx) for i in range(gx)]) for k in range(1, gx)]
+    returned = [lax.ppermute(results[1 + k], "gx", [(i, i ^ k) for i in range(gx)]) for k in range(gx - 1, 0, -1)]
     temperature = pl.pallas_call(
         functools.partial(merge_kernel, gy),
         out_shape=struct(layers, rows, LANES),

time: 33.9 us -> 35 us (1.032)
  starting transfers between devices: 13 us -> 15.1 us
  waiting for transfers between devices: 8.36 us -> 7.51 us
    ppermute x6 -> x7, starting transfers between devices: 10.3 us -> 12.3 us  [the longest x2 4.57 us: local(): lax.ppermute(only, 'gx', [(i, i ^ k) for i in range(gx) if abs(i - (i ^ k...]
    ppermute x6 -> x7, waiting for transfers between devices: 7.8 us -> 6.99 us  [the longest x2 5.04 us: local(): lax.ppermute(only, 'gx', [(i, i ^ k) for i in range(gx) if abs(i - (i ^ k...]
  transfers between devices with their start and end apart: 10 -> 11, of which waited for: 4 -> 5; matrix products, arithmetic and copies ran while one was open for 0% -> 0% of each run, Pallas kernels for 22% -> 21%
where the time goes in v1:
time: 35 us; the launch traced here: 34.8 us
  starting transfers between devices  15.1 us (43%)
  Pallas kernels  10.9 us (31%)
  waiting for transfers between devices  7.51 us (21%)
  between operations  0.71 us (2%)
  other arithmetic  0.63 us (2%)
    pallas_call x1, Pallas kernels, local(): pl.pallas_call(functools.partial(tile_kernel, gx, gy, shape), out_shape=(...  5.42 us
    ppermute x2, waiting for transfers between devices, local(): lax.ppermute(only, 'gx', [(i, i ^ k) for i in range(gx) if abs(i - (i ^ k...  5.04 us
    ppermute x2, starting transfers between devices, local(): lax.ppermute(only, 'gx', [(i, i ^ k) for i in range(gx) if abs(i - (i ^ k...  4.57 us
    ppermute x3, starting transfers between devices, local(): lax.ppermute(results[1 + k], 'gx', [(i, i ^ k) for i in range(gx)])  4.45 us
    ppermute x1, starting transfers between devices, local(): lax.ppermute(to_even, 'gx', even)  2.65 us
    pallas_call x1, Pallas kernels, local(): pl.pallas_call(functools.partial(pack_kernel, shape), out_shape=(struct(R...  2.01 us
    ppermute x3, waiting for transfers between devices, local(): lax.ppermute(results[1 + k], 'gx', [(i, i ^ k) for i in range(gx)])  1.94 us
    ppermute x1, starting transfers between devices, local(): across.append(lax.ppermute(value, ('gy', 'gz'), both))  1.6 us
  transfers between devices with their start and end apart: 11, of which 5 were waited for; matrix products, arithmetic and copies ran while one was open for 0% of the time, Pallas kernels for 21%

profile of v1, /device:TPU:0, one launch (start us, length us, event | category | flops | bytes accessed | tf_op | source)
XLA Modules:
  0.0 34.8 jit_solution(7617762642431241205)
XLA Ops:
  0.6 2.0 %pack.1 = (f32[2624,128]{1,0:T(8,128)S(1)}, f32[224,128]{1,0:T(8,128)S(1)}, f32[224,128]{1,0:T(8,128)S(1)}, f32[64,128]{1,0:T(8,128)S(1)}, s32[4,128]{1,0:T(4,12...) custom-call(f32[512,128]{1,0:T(8,128)} %bitcast.10, f32[512,128]{1,0:T(8,128)} %bitcast.11, f32[512,128]{1,0:T(8,128)} %bitcast.12, ...), custom_call_target="tpu_custom_call" | custom-call | tf_op jit(solution)/shard_map/pack/pallas_call | solution.py:569
  2.7 0.5 %collective-permute-start.4 = (f32[2624,128]{1,0:T(8,128)S(1)}, f32[2624,128]{1,0:T(8,128)S(1)}, u32[]{:S(2)}, u32[]{:S(2)}) collective-permute-start(f32[2624,128]{1,0:T(8,128)S(1)} %get-tuple-element.21.refs_0_), channel_id=1, source_target_pairs={{0,1},{1,0},{2,3},{3,2},{4,5},{5,4},{6,7},{7,6},{8,9},{9,8},{10,11... | collective-permute-start | bytes 4030472 | tf_op jit(solution)/shard_map/ppermute | solution.py:586
  3.2 2.6 %collective-permute-start = (f32[224,128]{1,0:T(8,128)S(1)}, f32[224,128]{1,0:T(8,128)S(1)}, u32[]{:S(2)}, u32[]{:S(2)}) collective-permute-start(f32[224,128]{1,0:T(8,128)S(1)} %get-tuple-element.25), channel_id=1, source_target_pairs={{0,4},{4,0},{8,12},{12,8},{1,5},{5,1},{9,13},{13,9},{2,6},{6,2},{1... | collective-permute-start | bytes 344072 | tf_op jit(solution)/shard_map/ppermute | solution.py:589
  5.8 0.7 %collective-permute-start.1 = (f32[224,128]{1,0:T(8,128)S(1)}, f32[224,128]{1,0:T(8,128)S(1)}, u32[]{:S(2)}, u32[]{:S(2)}) collective-permute-start(f32[224,128]{1,0:T(8,128)S(1)} %get-tuple-element.26), channel_id=1, source_target_pairs={{4,8},{8,4},{5,9},{9,5},{6,10},{10,6},{7,11},{11,7},{20,24},{24,20... | collective-permute-start | bytes 344072 | tf_op jit(solution)/shard_map/ppermute | solution.py:589
  6.5 4.4 %collective-permute-start.3 = (f32[64,128]{1,0:T(8,128)S(1)}, f32[64,128]{1,0:T(8,128)S(1)}, u32[]{:S(2)}, u32[]{:S(2)}) collective-permute-start(f32[64,128]{1,0:T(8,128)S(1)} %get-tuple-element.27), channel_id=1, source_target_pairs={{0,12},{12,0},{1,13},{13,1},{2,14},{14,2},{3,15},{15,3},{16,28},{2... | collective-permute-start | bytes 98312 | tf_op jit(solution)/shard_map/ppermute | solution.py:592
  10.9 0.2 collective-permute-start.2
  11.1 3.1 %collective-permute-done.3.refs_7_ = f32[64,128]{1,0:T(8,128)S(1)} collective-permute-done((f32[64,128]{1,0:T(8,128)S(1)}, f32[64,128]{1,0:T(8,128)S(1)}, u32[]{:S(2)}, u32[]{:S(2)}) %collective-permute-start.3) | collective-permute-done | bytes 32800 | tf_op jit(solution)/shard_map/ppermute | solution.py:592
  14.1 2.0 %collective-permute-done.2.refs_6_ = f32[64,128]{1,0:T(8,128)S(1)} collective-permute-done((f32[64,128]{1,0:T(8,128)S(1)}, f32[64,128]{1,0:T(8,128)S(1)}, u32[]{:S(2)}, u32[]{:S(2)}) %collective-permute-start.2) | collective-permute-done | bytes 32800 | tf_op jit(solution)/shard_map/ppermute | solution.py:592
  16.1 0.1 collective-permute-start.5
  16.2 0.7 %fill_own.1 = (f32[35,128,128]{2,1,0:T(8,128)S(1)}, f32[256,128]{1,0:T(8,128)S(1)}, f32[128,8]{1,0:T(8,128)S(1)}, f32[256,128]{1,0:T(8,128)S(1)}) custom-call(f32[2624,128]{1,0:T(8,128)S(1)} %get-tuple-element.21.refs_0_, s32[4,128]{1,0:T(4,128)S(1)} %get-tuple-element.22.refs_1_, s32[4,128]{1,0:T(4,128)S(1)} %get-tuple-element.23.refs_2_, ...), custom_call_target="tpu_custom_call" | custom-call | bytes 4500000 | tf_op jit(solution)/shard_map/fill_own/pallas_call | solution.py:599
  16.9 1.6 %collective-permute-start.7 = (f32[256,128]{1,0:T(8,128)S(1)}, f32[256,128]{1,0:T(8,128)S(1)}, u32[]{:S(2)}, u32[]{:S(2)}) collective-permute-start(f32[256,128]{1,0:T(8,128)S(1)} %get-tuple-element.34), channel_id=1, source_target_pairs={{0,3},{1,2},{2,1},{3,0},{4,7},{5,6},{6,5},{7,4},{8,11},{9,10},{10,... | collective-permute-start | bytes 393224 | tf_op jit(solution)/shard_map/ppermute | solution.py:618
  18.5 0.5 %collective-permute-start.6 = (f32[256,128]{1,0:T(8,128)S(1)}, f32[256,128]{1,0:T(8,128)S(1)}, u32[]{:S(2)}, u32[]{:S(2)}) collective-permute-start(f32[256,128]{1,0:T(8,128)S(1)} %get-tuple-element.34), channel_id=1, source_target_pairs={{0,2},{2,0},{1,3},{3,1},{4,6},{6,4},{5,7},{7,5},{8,10},{10,8},{9,1... | collective-permute-start | bytes 393224 | tf_op jit(solution)/shard_map/ppermute | solution.py:614
  19.0 0.0 collective-permute-done.5.refs_4_
  19.0 0.0 collective-permute-done.4.refs_0_
  19.0 0.5 %fill_partner.1.refs_1_ = f32[35,128,128]{2,1,0:T(8,128)S(1)} custom-call(f32[2624,128]{1,0:T(8,128)S(1)} %collective-permute-done.4.refs_0_, s32[4,128]{1,0:T(4,128)S(1)} %get-tuple-element.22.refs_1_, s32[4,128]{1,0:T(4,128)S(1)} %get-tuple-element.23.refs_2_, s32[4,128]{1,0:T(4,128)S(1)} %get-tuple-element.24.refs_3_, ...), custom_call_target="tpu_custom_call" | custom-call | bytes 4500000 | tf_op jit(solution)/shard_map/fill_partner/pallas_call | solution.py:620
  19.6 5.4 %tile_sweeps.1 = (f32[4,128,128]{2,1,0:T(8,128)S(1)}, f32[2,128,128]{2,1,0:T(8,128)S(1)}, f32[72,8,128]{2,1,0:T(8,128)S(1)}) custom-call(f32[35,128,128]{2,1,0:T(8,128)S(1)} %get-tuple-element.28.refs_0_, f32[35,128,128]{2,1,0:T(8,128)S(1)} %fill_partner.1.refs_1_, f32[128,8]{1,0:T(8,128)S(1)} %get-tuple-element.29.refs_2_), custom_call_target="tpu_custom_call" | custom-call | bytes 21000000 | tf_op jit(solution)/shard_map/tile_sweeps/pallas_call | solution.py:633
  25.0 0.5 %collective-permute-done.6.refs_6_ = f32[256,128]{1,0:T(8,128)S(1)} collective-permute-done((f32[256,128]{1,0:T(8,128)S(1)}, f32[256,128]{1,0:T(8,128)S(1)}, u32[]{:S(2)}, u32[]{:S(2)}) %collective-permute-start.6) | collective-permute-done | bytes 131104 | tf_op jit(solution)/shard_map/ppermute | solution.py:614
  25.5 1.5 %edge_sweeps.1 = (f32[4,8,128]{2,1,0:T(8,128)S(1)}, f32[32,128]{1,0:T(8,128)S(1)}, f32[32,128]{1,0:T(8,128)S(1)}, f32[32,128]{1,0:T(8,128)S(1)}, f32[32,128]{1,0:T(8,128)S(1)}) custom-call(f32[35,128,128]{2,1,0:T(8,128)S(1)} %get-tuple-element.28.refs_0_, f32[35,128,128]{2,1,0:T(8,128)S(1)} %fill_partner.1.refs_1_, f32[128,8]{1,0:T(8,128)S(1)} %get-tuple-element.29.refs_2_, ...), custom_call_target="tpu_custom_call" | custom-call | bytes 4500000 | tf_op jit(solution)/shard_map/edge_sweeps/pallas_call | solution.py:648
  27.1 2.5 %collective-permute-start.8 = (f32[32,128]{1,0:T(8,128)S(1)}, f32[32,128]{1,0:T(8,128)S(1)}, u32[]{:S(2)}, u32[]{:S(2)}) collective-permute-start(f32[32,128]{1,0:T(8,128)S(1)} %get-tuple-element.37), channel_id=1, source_target_pairs={{0,12},{4,8},{8,4},{12,0},{1,13},{5,9},{9,5},{13,1},{2,14},{6,10},... | collective-permute-start | bytes 49160 | tf_op jit(solution)/shard_map/ppermute | solution.py:661
  29.5 2.0 %collective-permute-start.10 = (f32[32,128]{1,0:T(8,128)S(1)}, f32[32,128]{1,0:T(8,128)S(1)}, u32[]{:S(2)}, u32[]{:S(2)}) collective-permute-start(f32[32,128]{1,0:T(8,128)S(1)} %get-tuple-element.39), channel_id=1, source_target_pairs={{0,4},{4,0},{8,12},{12,8},{1,5},{5,1},{9,13},{13,9},{2,6},{6,2},{1... | collective-permute-start | bytes 49160 | tf_op jit(solution)/shard_map/ppermute | solution.py:661
  31.5 0.7 %merge.1 = f32[4,128,128]{2,1,0:T(8,128)} custom-call(f32[4,128,128]{2,1,0:T(8,128)S(1)} %get-tuple-element.30.whole_ref, f32[4,8,128]{2,1,0:T(8,128)S(1)} %get-tuple-element.35.heat_ref), custom_call_target="tpu_custom_call" | custom-call | bytes 3000000 | tf_op jit(solution)/shard_map/merge/pallas_call | solution.py:662
  32.2 0.4 %collective-permute-done.8 = f32[32,128]{1,0:T(8,128)S(1)} collective-permute-done((f32[32,128]{1,0:T(8,128)S(1)}, f32[32,128]{1,0:T(8,128)S(1)}, u32[]{:S(2)}, u32[]{:S(2)}) %collective-permute-start.8) | collective-permute-done | bytes 16416 | tf_op jit(solution)/shard_map/ppermute | solution.py:661
  32.7 1.5 %collective-permute-done.9 = f32[32,128]{1,0:T(8,128)S(1)} collective-permute-done((f32[32,128]{1,0:T(8,128)S(1)}, f32[32,128]{1,0:T(8,128)S(1)}, u32[]{:S(2)}, u32[]{:S(2)}) %collective-permute-start.9) | collective-permute-done | bytes 16416 | tf_op jit(solution)/shard_map/ppermute | solution.py:661
  34.2 0.6 %add_bitcast_fusion = f32[1,32,128]{2,1,0:T(8,128)} fusion(f32[32,128]{1,0:T(8,128)S(1)} %collective-permute-done.10, f32[32,128]{1,0:T(8,128)S(1)} %collective-permute-done.9, f32[32,128]{1,0:T(8,128)S(1)} %get-tuple-element.36, f32[32,128]{1,0:T(8,128)S(1)} %collective-permute-done.8), kind=kLoop, calls=%fused_computation.1 | loop fusion | flops 12288 | bytes 81920 | tf_op jit(solution)/shard_map/broadcast_in_dim | solution.py:673
  (6 shorter events, 0.0 us)
Async XLA Ops:
  2.7 16.4 %collective-permute-start.4 = (f32[2624,128]{1,0:T(8,128)S(1)}, f32[2624,128]{1,0:T(8,128)S(1)}, u32[]{:S(2)}, u32[]{:S(2)}) collective-permute-start(f32[2624,128]{1,0:T(8,128)S(1)} %get-tuple-element.21.refs_0_), channel_id=1, source_target_pairs={{0,1},{1,0},{2,3},{3,2},{4,5},{5,4},{6,7},{7,6},{8,9},{9,8},{10,11... | collective-permute-start | bytes 4030472 | tf_op jit(solution)/shard_map/ppermute | solution.py:586
  3.2 12.9 %collective-permute-start = (f32[224,128]{1,0:T(8,128)S(1)}, f32[224,128]{1,0:T(8,128)S(1)}, u32[]{:S(2)}, u32[]{:S(2)}) collective-permute-start(f32[224,128]{1,0:T(8,128)S(1)} %get-tuple-element.25), channel_id=1, source_target_pairs={{0,4},{4,0},{8,12},{12,8},{1,5},{5,1},{9,13},{13,9},{2,6},{6,2},{1... | collective-permute-start | bytes 344072 | tf_op jit(solution)/shard_map/ppermute | solution.py:589
  5.8 10.3 %collective-permute-start.1 = (f32[224,128]{1,0:T(8,128)S(1)}, f32[224,128]{1,0:T(8,128)S(1)}, u32[]{:S(2)}, u32[]{:S(2)}) collective-permute-start(f32[224,128]{1,0:T(8,128)S(1)} %get-tuple-element.26), channel_id=1, source_target_pairs={{4,8},{8,4},{5,9},{9,5},{6,10},{10,6},{7,11},{11,7},{20,24},{24,20... | collective-permute-start | bytes 344072 | tf_op jit(solution)/shard_map/ppermute | solution.py:589
  6.5 7.6 %collective-permute-start.3 = (f32[64,128]{1,0:T(8,128)S(1)}, f32[64,128]{1,0:T(8,128)S(1)}, u32[]{:S(2)}, u32[]{:S(2)}) collective-permute-start(f32[64,128]{1,0:T(8,128)S(1)} %get-tuple-element.27), channel_id=1, source_target_pairs={{0,12},{12,0},{1,13},{13,1},{2,14},{14,2},{3,15},{15,3},{16,28},{2... | collective-permute-start | bytes 98312 | tf_op jit(solution)/shard_map/ppermute | solution.py:592
  10.9 5.2 %collective-permute-start.2 = (f32[64,128]{1,0:T(8,128)S(1)}, f32[64,128]{1,0:T(8,128)S(1)}, u32[]{:S(2)}, u32[]{:S(2)}) collective-permute-start(f32[64,128]{1,0:T(8,128)S(1)} %get-tuple-element.27), channel_id=1, source_target_pairs={{0,8},{4,12},{8,0},{12,4},{1,9},{5,13},{9,1},{13,5},{2,10},{6,14},... | collective-permute-start | bytes 98312 | tf_op jit(solution)/shard_map/ppermute | solution.py:592
  16.1 2.9 %collective-permute-start.5 = (f32[576,128]{1,0:T(8,128)S(1)}, f32[576,128]{1,0:T(8,128)S(1)}, u32[]{:S(2)}, u32[]{:S(2)}) collective-permute-start(f32[576,128]{1,0:T(8,128)S(1)} %pad_maximum_fusion), channel_id=1, source_target_pairs={{0,1},{1,0},{2,3},{3,2},{4,5},{5,4},{6,7},{7,6},{8,9},{9,8},{10,11... | collective-permute-start | bytes 884744 | tf_op jit(solution)/shard_map/ppermute | solution.py:594
  16.9 8.1 %collective-permute-start.7 = (f32[256,128]{1,0:T(8,128)S(1)}, f32[256,128]{1,0:T(8,128)S(1)}, u32[]{:S(2)}, u32[]{:S(2)}) collective-permute-start(f32[256,128]{1,0:T(8,128)S(1)} %get-tuple-element.34), channel_id=1, source_target_pairs={{0,3},{1,2},{2,1},{3,0},{4,7},{5,6},{6,5},{7,4},{8,11},{9,10},{10,... | collective-permute-start | bytes 393224 | tf_op jit(solution)/shard_map/ppermute | solution.py:618
  18.5 7.0 %collective-permute-start.6 = (f32[256,128]{1,0:T(8,128)S(1)}, f32[256,128]{1,0:T(8,128)S(1)}, u32[]{:S(2)}, u32[]{:S(2)}) collective-permute-start(f32[256,128]{1,0:T(8,128)S(1)} %get-tuple-element.34), channel_id=1, source_target_pairs={{0,2},{2,0},{1,3},{3,1},{4,6},{6,4},{5,7},{7,5},{8,10},{10,8},{9,1... | collective-permute-start | bytes 393224 | tf_op jit(solution)/shard_map/ppermute | solution.py:614
  27.1 5.6 %collective-permute-start.8 = (f32[32,128]{1,0:T(8,128)S(1)}, f32[32,128]{1,0:T(8,128)S(1)}, u32[]{:S(2)}, u32[]{:S(2)}) collective-permute-start(f32[32,128]{1,0:T(8,128)S(1)} %get-tuple-element.37), channel_id=1, source_target_pairs={{0,12},{4,8},{8,4},{12,0},{1,13},{5,9},{9,5},{13,1},{2,14},{6,10},... | collective-permute-start | bytes 49160 | tf_op jit(solution)/shard_map/ppermute | solution.py:661
  29.5 4.6 %collective-permute-start.9 = (f32[32,128]{1,0:T(8,128)S(1)}, f32[32,128]{1,0:T(8,128)S(1)}, u32[]{:S(2)}, u32[]{:S(2)}) collective-permute-start(f32[32,128]{1,0:T(8,128)S(1)} %get-tuple-element.38), channel_id=1, source_target_pairs={{0,8},{4,12},{8,0},{12,4},{1,9},{5,13},{9,1},{13,5},{2,10},{6,14},... | collective-permute-start | bytes 49160 | tf_op jit(solution)/shard_map/ppermute | solution.py:661
  29.5 4.6 %collective-permute-start.10 = (f32[32,128]{1,0:T(8,128)S(1)}, f32[32,128]{1,0:T(8,128)S(1)}, u32[]{:S(2)}, u32[]{:S(2)}) collective-permute-start(f32[32,128]{1,0:T(8,128)S(1)} %get-tuple-element.39), channel_id=1, source_target_pairs={{0,4},{4,0},{8,12},{12,8},{1,5},{5,1},{9,13},{13,9},{2,6},{6,2},{1... | collective-permute-start | bytes 49160 | tf_op jit(solution)/shard_map/ppermute | solution.py:661
